TPU v7x, 512 devices: a whole 4x4x16 slice. The times are simulated.
512 devices in a mesh: mode: 32 (over y, z_hi, x), rows: 16 (over z_lo, core).
Axes of the slice: x: 4, y: 4, z: 16 (z_hi: 2, z_lo: 8; z = z_hi * 8 + z_lo), core: 2. Of those that a mesh axis runs over, the one named last changes fastest.
Arguments:
- tangents: float32 [128, 3, 128, 1024], P('mode', None, 'rows'), may hold values from -6 to 6
- checkpoints: float32 [8, 3, 128, 1024], P(None, None, 'rows', 'mode'), may hold values from 0 to 0.5
- owner_order: int32 [8], replicated, may hold values from 0 to 7, each once
- land_mask: int32 [128, 1024], P('rows'), may hold values 0 or 1
- coefficients: float32 [128, 128], replicated, may hold values from -0.9 to 0.9
Outputs:
- vectors: float32 [128, 3, 128, 1024], P(None, None, 'rows', 'mode')
Inputs may be any that keep to these rules, and one draw needn't show every extreme that they name: `owner_order`: every checkpoint slot is named by exactly one step.
All inputs are finite; a program needn't handle non-finite values. No bound on the sum of `land_mask` on one device may be relied on, other than what follows from the above.
Results may differ from a plain program's by a relative error of at most 0.0002.
Values sent between devices are 32-bit elements; how exact they have to be, the bound alone decides.
No kernel may reach another device: no remote copies, remote signals or barrier semaphores. Data moves between devices by JAX's collectives and lax.ppermute only.
A program may use at most 64 MiB of HBM per device.

v0:
```python
import jax
import jax.numpy as jnp
from jax import lax
from jax.sharding import PartitionSpec as P

mean_depth = 1.0
gravity = 1.0
coriolis = 0.5
time_step = 0.5


def padded(cells, sides, width):
    for axis, dim in sides:
        count = lax.axis_size(axis)
        ends = count - 1
        head = lax.slice_in_dim(cells, 0, width, axis=dim)
        tail = lax.slice_in_dim(cells, cells.shape[dim] - width, cells.shape[dim], axis=dim)
        cells = jnp.concatenate(
            [
                lax.ppermute(tail, axis, [(i, (i + 1) % count) for i in range(ends)]),
                cells,
                lax.ppermute(head, axis, [((i + 1) % count, i) for i in range(ends)]),
            ],
            axis=dim,
        )
    return cells


def deriv_x(values):
    return 0.5 * (jnp.roll(values, -1, -1) - jnp.roll(values, 1, -1))


def deriv_y(values):
    return 0.5 * (values[..., 2:, :] - values[..., :-2, :])


def interior(values):
    return values[..., 1:-1, :]


def tendency(base_flow, current):
    depth_total = mean_depth + base_flow[0]
    flow_u = base_flow[1]
    flow_v = base_flow[2]
    height = current[:, 0]
    zonal = current[:, 1]
    meridional = current[:, 2]
    flux_x = depth_total * zonal + height * flow_u
    flux_y = depth_total * meridional + height * flow_v
    height_rate = -(interior(deriv_x(flux_x)) + deriv_y(flux_y))
    zonal_mid = interior(zonal)
    merid_mid = interior(meridional)
    flow_umid = interior(flow_u)
    flow_vmid = interior(flow_v)
    zonal_rate = (
        -(
            flow_umid * interior(deriv_x(zonal))
            + zonal_mid * interior(deriv_x(flow_u))
            + flow_vmid * deriv_y(zonal)
            + merid_mid * deriv_y(flow_u)
        )
        + coriolis * merid_mid
        - gravity * interior(deriv_x(height))
    )
    merid_rate = (
        -(
            flow_umid * interior(deriv_x(meridional))
            + zonal_mid * interior(deriv_x(flow_v))
            + flow_vmid * deriv_y(meridional)
            + merid_mid * deriv_y(flow_v)
        )
        - coriolis * zonal_mid
        - gravity * deriv_y(height)
    )
    return jnp.stack([height_rate, zonal_rate, merid_rate], 1)


def on_device(tangents, checkpoints, owner_order, land_mask, coefficients):
    wet_mask = land_mask.astype(jnp.float32)
    current = wet_mask * tangents
    depth = 1
    flows_wide, wet_stack = (
        padded(checkpoints, (("rows", 2),), depth),
        padded(wet_mask[None, None], (("rows", 2),), depth),
    )

    def fetch_flow(step_index):
        held_tile = lax.dynamic_index_in_dim(flows_wide, owner_order[step_index], 0, keepdims=False)
        return lax.all_gather(held_tile, "mode", axis=2, tiled=True)

    total_steps = owner_order.shape[0]

    def advance(step_index, current):
        base_wide = fetch_flow(step_index)
        widened = padded(current, (("rows", 2),), 1)
        slope_one = tendency(base_wide, widened)
        middle = wet_mask * (current + time_step * slope_one)
        middle_wide = padded(middle, (("rows", 2),), 1)
        slope_two = tendency(base_wide, middle_wide)
        return wet_mask * (current + 0.5 * time_step * (slope_one + slope_two))

    final = lax.fori_loop(0, total_steps, advance, current)
    mixing = jnp.eye(coefficients.shape[0], dtype=jnp.float32) + jnp.triu(coefficients)
    cell_block = lax.all_to_all(final, "mode", split_axis=3, concat_axis=0, tiled=True)
    flattened = cell_block.reshape(cell_block.shape[0], -1)
    mixed = jnp.dot(
        mixing.T, flattened, precision=lax.Precision.HIGHEST, preferred_element_type=jnp.float32
    )
    return mixed.reshape(cell_block.shape)


def solution(mesh):
    placed = (
        P("mode", None, "rows", None),
        P(None, None, "rows", "mode"),
        P(),
        P("rows", None),
        P(),
    )
    return jax.shard_map(
        on_device,
        mesh=mesh,
        in_specs=placed,
        out_specs=P(None, None, "rows", "mode"),
        check_vma=False,
    )
```

profile of v0, /device:TPU:97, one launch (start us, length us, event | category | flops | bytes accessed | tf_op | source)
XLA Modules:
  0.0 1700.1 jit_solution(5932026285515117026)
XLA Ops:
  0.9 5.3 collective-permute-start.4
  13.1 1625.2 %while.13 = (s32[]{:T(128)}, f32[4,3,8,1024]{3,2,1,0:T(8,128)S(1)}, f32[8,1024]{1,0:T(8,128)}, s32[8]{0:T(128)}, f32[8,3,10,32]{3,0,2,1:T(8,128)}, /*index=5*/s32[]{:T(128)}, s32[]{:T(128)}, s32[]{:T(128)}) while((s32[]{:T(128)}, f32[4,3,8,1024]{3,2,1,0:T(8,128)S(1)}, f32[8,1024]{1,0:T(8,128)}, s32[8]{0:T(128)}, f32[8,3,10,32]{3,0,2,1:T(8,128)}, ...), condition=%wide.region_1.2_spmd, body=%wide.region_0.1_spmd.sunk | while | flops 5195781 | bytes 25504440 | solution.py:102
  15.8 4.9 collective-permute-start.1
  24.9 165.8 %all-gather.2 = f32[1,3,10,1024]{2,0,1,3:T(1,128)S(1)} all-gather(f32[1,3,10,32]{2,0,1,3:T(1,128)S(1)} %copy.138), channel_id=2, replica_groups=mesh['mode'=32,'rows'=16] {'mode'}, dimensions={3}, use_global_device_ids=true | all-gather | bytes 126720 | tf_op jit(solution)/shard_map/while/body/eval_jaxpr/all_gather | solution.py:89
  204.9 16.6 collective-permute-start.2
  221.5 29.6 %collective-permute-start.3 = (f32[4,3,1,1024]{3,2,0,1:T(1,128)S(1)}, f32[4,3,1,1024]{3,2,0,1:T(1,128)S(1)}, u32[]{:S(2)}, u32[]{:S(2)}) collective-permute-start(f32[4,3,1,1024]{3,2,0,1:T(1,128)S(1)} %get-tuple-element.330), channel_id=1, source_target_pairs={{0,1},{1,2},{2,3},{3,4},{4,5},{5,6},{6,7},{7,8},{8,9},{9,10},{10,1... | collective-permute-start | bytes 147464 | tf_op jit(solution)/shard_map/while/body/eval_jaxpr/ppermute | solution.py:20
  256.8 5.5 collective-permute-start.1
  266.5 151.1 %all-gather.2 = f32[1,3,10,1024]{2,0,1,3:T(1,128)S(1)} all-gather(f32[1,3,10,32]{2,0,1,3:T(1,128)S(1)} %copy.138), channel_id=2, replica_groups=mesh['mode'=32,'rows'=16] {'mode'}, dimensions={3}, use_global_device_ids=true | all-gather | bytes 126720 | tf_op jit(solution)/shard_map/while/body/eval_jaxpr/all_gather | solution.py:89
  431.8 7.8 collective-permute-start.2
  439.6 15.1 collective-permute-start.3
  460.4 5.6 collective-permute-start.1
  470.2 151.9 %all-gather.2 = f32[1,3,10,1024]{2,0,1,3:T(1,128)S(1)} all-gather(f32[1,3,10,32]{2,0,1,3:T(1,128)S(1)} %copy.138), channel_id=2, replica_groups=mesh['mode'=32,'rows'=16] {'mode'}, dimensions={3}, use_global_device_ids=true | all-gather | bytes 126720 | tf_op jit(solution)/shard_map/while/body/eval_jaxpr/all_gather | solution.py:89
  636.3 11.9 collective-permute-start.2
  653.9 4.2 collective-permute-start
  665.4 150.4 %all-gather.2 = f32[1,3,10,1024]{2,0,1,3:T(1,128)S(1)} all-gather(f32[1,3,10,32]{2,0,1,3:T(1,128)S(1)} %copy.138), channel_id=2, replica_groups=mesh['mode'=32,'rows'=16] {'mode'}, dimensions={3}, use_global_device_ids=true | all-gather | bytes 126720 | tf_op jit(solution)/shard_map/while/body/eval_jaxpr/all_gather | solution.py:89
  830.2 10.3 collective-permute-start.2
  857.7 161.2 %all-gather.2 = f32[1,3,10,1024]{2,0,1,3:T(1,128)S(1)} all-gather(f32[1,3,10,32]{2,0,1,3:T(1,128)S(1)} %copy.138), channel_id=2, replica_groups=mesh['mode'=32,'rows'=16] {'mode'}, dimensions={3}, use_global_device_ids=true | all-gather | bytes 126720 | tf_op jit(solution)/shard_map/while/body/eval_jaxpr/all_gather | solution.py:89
  1033.1 8.1 collective-permute-start.2
  1046.9 4.2 collective-permute-start
  1058.5 153.6 %all-gather.2 = f32[1,3,10,1024]{2,0,1,3:T(1,128)S(1)} all-gather(f32[1,3,10,32]{2,0,1,3:T(1,128)S(1)} %copy.138), channel_id=2, replica_groups=mesh['mode'=32,'rows'=16] {'mode'}, dimensions={3}, use_global_device_ids=true | all-gather | bytes 126720 | tf_op jit(solution)/shard_map/while/body/eval_jaxpr/all_gather | solution.py:89
  1226.4 9.9 collective-permute-start.2
  1242.0 4.2 collective-permute-start
  1253.5 162.1 %all-gather.2 = f32[1,3,10,1024]{2,0,1,3:T(1,128)S(1)} all-gather(f32[1,3,10,32]{2,0,1,3:T(1,128)S(1)} %copy.138), channel_id=2, replica_groups=mesh['mode'=32,'rows'=16] {'mode'}, dimensions={3}, use_global_device_ids=true | all-gather | bytes 126720 | tf_op jit(solution)/shard_map/while/body/eval_jaxpr/all_gather | solution.py:89
  1429.9 4.6 collective-permute-start.2
  1452.0 155.2 %all-gather.2 = f32[1,3,10,1024]{2,0,1,3:T(1,128)S(1)} all-gather(f32[1,3,10,32]{2,0,1,3:T(1,128)S(1)} %copy.138), channel_id=2, replica_groups=mesh['mode'=32,'rows'=16] {'mode'}, dimensions={3}, use_global_device_ids=true | all-gather | bytes 126720 | tf_op jit(solution)/shard_map/while/body/eval_jaxpr/all_gather | solution.py:89
  1621.4 6.3 collective-permute-start.2
  1627.8 7.6 collective-permute-start.3
  1638.4 4.6 copy.94
  1642.9 9.3 reshape.31
  1656.3 24.8 %all-to-all-done = f32[32,1,3072]{2,1,0:T(1,128)S(1)} async-done(((f32[32,1,3072]{2,1,0:T(1,128)}), f32[32,1,3072]{2,1,0:T(1,128)S(1)}, u32[]{:S(2)}, u32[]{:S(2)}) %all-to-all-start) | async-done | bytes 393248 | tf_op jit(solution)/shard_map/all_to_all | solution.py:104
  1683.2 9.2 reshape.32
  1692.4 5.6 copy.95
  (570 shorter events, 216.0 us)
Async XLA Ops:
  0.9 9.7 collective-permute-start.4
  6.3 6.2 collective-permute-start.5
  13.9 188.2 %collective-permute-start = (f32[4,3,1,1024]{3,2,0,1:T(1,128)}, f32[4,3,1,1024]{3,2,0,1:T(1,128)}, u32[]{:S(2)}, u32[]{:S(2)}) collective-permute-start(f32[4,3,1,1024]{3,2,0,1:T(1,128)} %get-tuple-element.286), channel_id=1, source_target_pairs={{1,0},{2,1},{3,2},{4,3},{5,4},{6,5},{7,6},{8,7},{9,8},{10,9},{11,1... | collective-permute-start | bytes 147464 | tf_op jit(solution)/shard_map/while/body/eval_jaxpr/ppermute | solution.py:22
  15.8 186.2 %collective-permute-start.1 = (f32[4,3,1,1024]{3,2,0,1:T(1,128)}, f32[4,3,1,1024]{3,2,0,1:T(1,128)}, u32[]{:S(2)}, u32[]{:S(2)}) collective-permute-start(f32[4,3,1,1024]{3,2,0,1:T(1,128)} %get-tuple-element.287), channel_id=1, source_target_pairs={{0,1},{1,2},{2,3},{3,4},{4,5},{5,6},{6,7},{7,8},{8,9},{9,10},{10,1... | collective-permute-start | bytes 147464 | tf_op jit(solution)/shard_map/while/body/eval_jaxpr/ppermute | solution.py:20
  204.9 46.2 %collective-permute-start.2 = (f32[4,3,1,1024]{3,2,0,1:T(1,128)S(1)}, f32[4,3,1,1024]{3,2,0,1:T(1,128)S(1)}, u32[]{:S(2)}, u32[]{:S(2)}) collective-permute-start(f32[4,3,1,1024]{3,2,0,1:T(1,128)S(1)} %get-tuple-element.329), channel_id=1, source_target_pairs={{1,0},{2,1},{3,2},{4,3},{5,4},{6,5},{7,6},{8,7},{9,8},{10,9},{11,1... | collective-permute-start | bytes 147464 | tf_op jit(solution)/shard_map/while/body/eval_jaxpr/ppermute | solution.py:22
  221.5 30.8 %collective-permute-start.3 = (f32[4,3,1,1024]{3,2,0,1:T(1,128)S(1)}, f32[4,3,1,1024]{3,2,0,1:T(1,128)S(1)}, u32[]{:S(2)}, u32[]{:S(2)}) collective-permute-start(f32[4,3,1,1024]{3,2,0,1:T(1,128)S(1)} %get-tuple-element.330), channel_id=1, source_target_pairs={{0,1},{1,2},{2,3},{3,4},{4,5},{5,6},{6,7},{7,8},{8,9},{9,10},{10,1... | collective-permute-start | bytes 147464 | tf_op jit(solution)/shard_map/while/body/eval_jaxpr/ppermute | solution.py:20
  254.9 174.1 %collective-permute-start = (f32[4,3,1,1024]{3,2,0,1:T(1,128)}, f32[4,3,1,1024]{3,2,0,1:T(1,128)}, u32[]{:S(2)}, u32[]{:S(2)}) collective-permute-start(f32[4,3,1,1024]{3,2,0,1:T(1,128)} %get-tuple-element.286), channel_id=1, source_target_pairs={{1,0},{2,1},{3,2},{4,3},{5,4},{6,5},{7,6},{8,7},{9,8},{10,9},{11,1... | collective-permute-start | bytes 147464 | tf_op jit(solution)/shard_map/while/body/eval_jaxpr/ppermute | solution.py:22
  256.8 172.2 %collective-permute-start.1 = (f32[4,3,1,1024]{3,2,0,1:T(1,128)}, f32[4,3,1,1024]{3,2,0,1:T(1,128)}, u32[]{:S(2)}, u32[]{:S(2)}) collective-permute-start(f32[4,3,1,1024]{3,2,0,1:T(1,128)} %get-tuple-element.287), channel_id=1, source_target_pairs={{0,1},{1,2},{2,3},{3,4},{4,5},{5,6},{6,7},{7,8},{8,9},{9,10},{10,1... | collective-permute-start | bytes 147464 | tf_op jit(solution)/shard_map/while/body/eval_jaxpr/ppermute | solution.py:20
  431.8 22.9 %collective-permute-start.2 = (f32[4,3,1,1024]{3,2,0,1:T(1,128)S(1)}, f32[4,3,1,1024]{3,2,0,1:T(1,128)S(1)}, u32[]{:S(2)}, u32[]{:S(2)}) collective-permute-start(f32[4,3,1,1024]{3,2,0,1:T(1,128)S(1)} %get-tuple-element.329), channel_id=1, source_target_pairs={{1,0},{2,1},{3,2},{4,3},{5,4},{6,5},{7,6},{8,7},{9,8},{10,9},{11,1... | collective-permute-start | bytes 147464 | tf_op jit(solution)/shard_map/while/body/eval_jaxpr/ppermute | solution.py:22
  439.6 16.3 collective-permute-start.3
  458.4 175.0 %collective-permute-start = (f32[4,3,1,1024]{3,2,0,1:T(1,128)}, f32[4,3,1,1024]{3,2,0,1:T(1,128)}, u32[]{:S(2)}, u32[]{:S(2)}) collective-permute-start(f32[4,3,1,1024]{3,2,0,1:T(1,128)} %get-tuple-element.286), channel_id=1, source_target_pairs={{1,0},{2,1},{3,2},{4,3},{5,4},{6,5},{7,6},{8,7},{9,8},{10,9},{11,1... | collective-permute-start | bytes 147464 | tf_op jit(solution)/shard_map/while/body/eval_jaxpr/ppermute | solution.py:22
  460.4 173.1 %collective-permute-start.1 = (f32[4,3,1,1024]{3,2,0,1:T(1,128)}, f32[4,3,1,1024]{3,2,0,1:T(1,128)}, u32[]{:S(2)}, u32[]{:S(2)}) collective-permute-start(f32[4,3,1,1024]{3,2,0,1:T(1,128)} %get-tuple-element.287), channel_id=1, source_target_pairs={{0,1},{1,2},{2,3},{3,4},{4,5},{5,6},{6,7},{7,8},{8,9},{9,10},{10,1... | collective-permute-start | bytes 147464 | tf_op jit(solution)/shard_map/while/body/eval_jaxpr/ppermute | solution.py:20
  636.3 13.8 collective-permute-start.2
  648.2 3.1 collective-permute-start.3
  653.9 173.4 %collective-permute-start = (f32[4,3,1,1024]{3,2,0,1:T(1,128)}, f32[4,3,1,1024]{3,2,0,1:T(1,128)}, u32[]{:S(2)}, u32[]{:S(2)}) collective-permute-start(f32[4,3,1,1024]{3,2,0,1:T(1,128)} %get-tuple-element.286), channel_id=1, source_target_pairs={{1,0},{2,1},{3,2},{4,3},{5,4},{6,5},{7,6},{8,7},{9,8},{10,9},{11,1... | collective-permute-start | bytes 147464 | tf_op jit(solution)/shard_map/while/body/eval_jaxpr/ppermute | solution.py:22
  658.1 169.2 %collective-permute-start.1 = (f32[4,3,1,1024]{3,2,0,1:T(1,128)}, f32[4,3,1,1024]{3,2,0,1:T(1,128)}, u32[]{:S(2)}, u32[]{:S(2)}) collective-permute-start(f32[4,3,1,1024]{3,2,0,1:T(1,128)} %get-tuple-element.287), channel_id=1, source_target_pairs={{0,1},{1,2},{2,3},{3,4},{4,5},{5,6},{6,7},{7,8},{8,9},{9,10},{10,1... | collective-permute-start | bytes 147464 | tf_op jit(solution)/shard_map/while/body/eval_jaxpr/ppermute | solution.py:20
  830.2 12.2 collective-permute-start.2
  846.1 184.1 %collective-permute-start = (f32[4,3,1,1024]{3,2,0,1:T(1,128)}, f32[4,3,1,1024]{3,2,0,1:T(1,128)}, u32[]{:S(2)}, u32[]{:S(2)}) collective-permute-start(f32[4,3,1,1024]{3,2,0,1:T(1,128)} %get-tuple-element.286), channel_id=1, source_target_pairs={{1,0},{2,1},{3,2},{4,3},{5,4},{6,5},{7,6},{8,7},{9,8},{10,9},{11,1... | collective-permute-start | bytes 147464 | tf_op jit(solution)/shard_map/while/body/eval_jaxpr/ppermute | solution.py:22
  850.3 179.9 %collective-permute-start.1 = (f32[4,3,1,1024]{3,2,0,1:T(1,128)}, f32[4,3,1,1024]{3,2,0,1:T(1,128)}, u32[]{:S(2)}, u32[]{:S(2)}) collective-permute-start(f32[4,3,1,1024]{3,2,0,1:T(1,128)} %get-tuple-element.287), channel_id=1, source_target_pairs={{0,1},{1,2},{2,3},{3,4},{4,5},{5,6},{6,7},{7,8},{8,9},{9,10},{10,1... | collective-permute-start | bytes 147464 | tf_op jit(solution)/shard_map/while/body/eval_jaxpr/ppermute | solution.py:20
  1033.1 10.0 collective-permute-start.2
  1046.9 176.6 %collective-permute-start = (f32[4,3,1,1024]{3,2,0,1:T(1,128)}, f32[4,3,1,1024]{3,2,0,1:T(1,128)}, u32[]{:S(2)}, u32[]{:S(2)}) collective-permute-start(f32[4,3,1,1024]{3,2,0,1:T(1,128)} %get-tuple-element.286), channel_id=1, source_target_pairs={{1,0},{2,1},{3,2},{4,3},{5,4},{6,5},{7,6},{8,7},{9,8},{10,9},{11,1... | collective-permute-start | bytes 147464 | tf_op jit(solution)/shard_map/while/body/eval_jaxpr/ppermute | solution.py:22
  1051.1 172.4 %collective-permute-start.1 = (f32[4,3,1,1024]{3,2,0,1:T(1,128)}, f32[4,3,1,1024]{3,2,0,1:T(1,128)}, u32[]{:S(2)}, u32[]{:S(2)}) collective-permute-start(f32[4,3,1,1024]{3,2,0,1:T(1,128)} %get-tuple-element.287), channel_id=1, source_target_pairs={{0,1},{1,2},{2,3},{3,4},{4,5},{5,6},{6,7},{7,8},{8,9},{9,10},{10,1... | collective-permute-start | bytes 147464 | tf_op jit(solution)/shard_map/while/body/eval_jaxpr/ppermute | solution.py:20
  1226.4 11.8 collective-permute-start.2
  1242.0 185.0 %collective-permute-start = (f32[4,3,1,1024]{3,2,0,1:T(1,128)}, f32[4,3,1,1024]{3,2,0,1:T(1,128)}, u32[]{:S(2)}, u32[]{:S(2)}) collective-permute-start(f32[4,3,1,1024]{3,2,0,1:T(1,128)} %get-tuple-element.286), channel_id=1, source_target_pairs={{1,0},{2,1},{3,2},{4,3},{5,4},{6,5},{7,6},{8,7},{9,8},{10,9},{11,1... | collective-permute-start | bytes 147464 | tf_op jit(solution)/shard_map/while/body/eval_jaxpr/ppermute | solution.py:22
  1246.2 180.8 %collective-permute-start.1 = (f32[4,3,1,1024]{3,2,0,1:T(1,128)}, f32[4,3,1,1024]{3,2,0,1:T(1,128)}, u32[]{:S(2)}, u32[]{:S(2)}) collective-permute-start(f32[4,3,1,1024]{3,2,0,1:T(1,128)} %get-tuple-element.287), channel_id=1, source_target_pairs={{0,1},{1,2},{2,3},{3,4},{4,5},{5,6},{6,7},{7,8},{8,9},{9,10},{10,1... | collective-permute-start | bytes 147464 | tf_op jit(solution)/shard_map/while/body/eval_jaxpr/ppermute | solution.py:20
  1429.9 6.8 collective-permute-start.2
  1434.5 3.3 collective-permute-start.3
  1440.4 178.2 %collective-permute-start = (f32[4,3,1,1024]{3,2,0,1:T(1,128)}, f32[4,3,1,1024]{3,2,0,1:T(1,128)}, u32[]{:S(2)}, u32[]{:S(2)}) collective-permute-start(f32[4,3,1,1024]{3,2,0,1:T(1,128)} %get-tuple-element.286), channel_id=1, source_target_pairs={{1,0},{2,1},{3,2},{4,3},{5,4},{6,5},{7,6},{8,7},{9,8},{10,9},{11,1... | collective-permute-start | bytes 147464 | tf_op jit(solution)/shard_map/while/body/eval_jaxpr/ppermute | solution.py:22
  1444.4 174.1 %collective-permute-start.1 = (f32[4,3,1,1024]{3,2,0,1:T(1,128)}, f32[4,3,1,1024]{3,2,0,1:T(1,128)}, u32[]{:S(2)}, u32[]{:S(2)}) collective-permute-start(f32[4,3,1,1024]{3,2,0,1:T(1,128)} %get-tuple-element.287), channel_id=1, source_target_pairs={{0,1},{1,2},{2,3},{3,4},{4,5},{5,6},{6,7},{7,8},{8,9},{9,10},{10,1... | collective-permute-start | bytes 147464 | tf_op jit(solution)/shard_map/while/body/eval_jaxpr/ppermute | solution.py:20
  1621.4 13.9 collective-permute-start.2
  1627.8 8.8 collective-permute-start.3
  1652.3 28.8 %all-to-all-start = ((f32[32,1,3072]{2,1,0:T(1,128)}), f32[32,1,3072]{2,1,0:T(1,128)S(1)}, u32[]{:S(2)}, u32[]{:S(2)}) async-start(f32[32,1,3072]{2,1,0:T(1,128)} %reshape.31), calls=%async_computation | async-start | bytes 786432 | tf_op jit(solution)/shard_map/all_to_all | solution.py:104
  (37 other events, 71.5 us)
where the time goes:
time: 1700 us
  blocking collectives  1250 us (74%)
  starting transfers between devices  207 us (12%)
  local copies, waits for them, and re-layouts  139 us (8%)
  other arithmetic  47.6 us (3%)
  waiting for transfers between devices  36 us (2%)
  loops' own time  17.7 us (1%)
    all_gather x8, blocking collectives, fetch_flow(): return lax.all_gather(held_tile, 'mode', axis=2, tiled=True)  1250 us
    ppermute x17, starting transfers between devices, padded(): lax.ppermute(head, axis, [((i + 1) % count, i) for i in range(ends)])  104 us
    ppermute x17, starting transfers between devices, padded(): lax.ppermute(tail, axis, [(i, (i + 1) % count) for i in range(ends)])  99.2 us
    slice x208, local copies, waits for them, and re-layouts, deriv_x(): return 0.5 * (jnp.roll(values, -1, -1) - jnp.roll(values, 1, -1))  49.1 us
  transfers between devices with their start and end apart: 35, of which 10 were waited for; matrix products, arithmetic and copies ran while one was open for 7% of the time, Pallas kernels for 0%

commit v1 on v0

--- a/solution.py
+++ b/solution.py
@@ -86,7 +86,9 @@
 
     def fetch_flow(step_index):
         held_tile = lax.dynamic_index_in_dim(flows_wide, owner_order[step_index], 0, keepdims=False)
-        return lax.all_gather(held_tile, "mode", axis=2, tiled=True)
+        return jnp.concatenate(
+            lax.all_to_all(jnp.stack([held_tile] * lax.axis_size("mode")), "mode", 0, 0), axis=2
+        )
 
     total_steps = owner_order.shape[0]
 

time: 1700 us -> 586 us (0.34)
  blocking collectives: 1250 us -> 0 us
  waiting for transfers between devices: 36 us -> 136 us
  starting transfers between devices: 207 us -> 169 us
  local copies, waits for them, and re-layouts: 139 us -> 175 us
  other arithmetic: 47.6 us -> 80.8 us
    all_gather x8 -> x0, blocking collectives: 1250 us -> none  [fetch_flow(): return lax.all_gather(held_tile, 'mode', axis=2, tiled=True)]
    all_to_all x0 -> x8, waiting for transfers between devices: none -> 104 us  [fetch_flow(): lax.all_to_all(jnp.stack([held_tile] * lax.axis_size('mode')), 'mode', 0, 0)]
    ppermute x17, starting transfers between devices: 104 us -> 32.8 us  [padded(): lax.ppermute(head, axis, [((i + 1) % count, i) for i in range(ends)])]
    all_to_all x0 -> x8, starting transfers between devices: none -> 42.8 us  [fetch_flow(): lax.all_to_all(jnp.stack([held_tile] * lax.axis_size('mode')), 'mode', 0, 0)]
    mul x0 -> x32, local copies, waits for them, and re-layouts: none -> 32.4 us  [the longest x16 16.1 us: deriv_y(): return 0.5 * (values[..., 2:, :] - values[..., :-2, :])]
    all_gather x8 -> x0, local copies, waits for them, and re-layouts: 24.7 us -> none  [fetch_flow(): return lax.all_gather(held_tile, 'mode', axis=2, tiled=True)]
    another operation x56, other arithmetic: 8.18 us -> 31.4 us  [tendency(): return jnp.stack([height_rate, zonal_rate, merid_rate], 1)]
    slice x208 -> x144, local copies, waits for them, and re-layouts: 49.1 us -> 53.2 us  [deriv_x(): return 0.5 * (jnp.roll(values, -1, -1) - jnp.roll(values, 1, -1))]
  transfers between devices with their start and end apart: 35 -> 43, of which waited for: 10 -> 18; matrix products, arithmetic and copies ran while one was open for 7% -> 10% of each run, Pallas kernels for 0% -> 0%
where the time goes in v1:
time: 586 us; the launch traced here: 580 us
  local copies, waits for them, and re-layouts  175 us (30%)
  starting transfers between devices  169 us (29%)
  waiting for transfers between devices  136 us (23%)
  other arithmetic  80.8 us (14%)
  loops' own time  17.9 us (3%)
    all_to_all x8, waiting for transfers between devices, fetch_flow(): lax.all_to_all(jnp.stack([held_tile] * lax.axis_size('mode')), 'mode', 0, 0)  104 us
    ppermute x17, starting transfers between devices, padded(): lax.ppermute(tail, axis, [(i, (i + 1) % count) for i in range(ends)])  89.1 us
    slice x144, local copies, waits for them, and re-layouts, deriv_x(): return 0.5 * (jnp.roll(values, -1, -1) - jnp.roll(values, 1, -1))  53.2 us
    all_to_all x8, starting transfers between devices, fetch_flow(): lax.all_to_all(jnp.stack([held_tile] * lax.axis_size('mode')), 'mode', 0, 0)  42.8 us
    ppermute x17, starting transfers between devices, padded(): lax.ppermute(head, axis, [((i + 1) % count, i) for i in range(ends)])  32.8 us
    another operation x56, other arithmetic, tendency(): return jnp.stack([height_rate, zonal_rate, merid_rate], 1)  31.4 us
    all_to_all x1, waiting for transfers between devices, on_device(): lax.all_to_all(final, 'mode', split_axis=3, concat_axis=0, tiled=True)  21.5 us
    unnamed x7, local copies, waits for them, and re-layouts  20.1 us
  transfers between devices with their start and end apart: 43, of which 18 were waited for; matrix products, arithmetic and copies ran while one was open for 10% of the time, Pallas kernels for 0%

profile of v1, /device:TPU:97, one launch (start us, length us, event | category | flops | bytes accessed | tf_op | source)
XLA Modules:
  0.0 580.3 jit_solution(18049364817378683403)
XLA Ops:
  0.9 5.3 collective-permute-start.4
  13.3 508.8 %while.13 = (s32[]{:T(128)}, f32[4,3,8,1024]{3,2,1,0:T(8,128)S(1)}, f32[8,1024]{1,0:T(8,128)}, s32[8]{0:T(128)}, f32[8,3,10,32]{3,1,2,0:T(4,128)}, /*index=5*/s32[]{:T(128)}, s32[]{:T(128)}, s32[]{:T(128)}, f32[]{:T(128)}) while((s32[]{:T(128)}, f32[4,3,8,1024]{3,2,1,0:T(8,128)S(1)}, f32[8,1024]{1,0:T(8,128)}, s32[8]{0:T(128)}, ...), condition=%wide.region_1.2_spmd, body=%wide.region_0.1_spmd.sunk | while | flops 5195781 | bytes 28583172 | solution.py:104
  15.2 4.9 collective-permute-start.1
  25.2 15.5 %all-to-all-start = ((f32[32,1,960]{2,1,0:T(1,128)}), f32[32,1,960]{2,1,0:T(1,128)S(1)}, u32[]{:S(2)}, u32[]{:S(2)}) async-start(f32[32,1,960]{2,1,0:T(1,128)} %reshape.94), calls=%async_computation | async-start | bytes 262144 | tf_op jit(solution)/shard_map/while/body/eval_jaxpr/all_to_all | solution.py:90
  44.3 13.8 %all-to-all-done = f32[32,1,960]{2,1,0:T(1,128)S(1)} async-done(((f32[32,1,960]{2,1,0:T(1,128)}), f32[32,1,960]{2,1,0:T(1,128)S(1)}, u32[]{:S(2)}, u32[]{:S(2)}) %all-to-all-start) | async-done | bytes 122912 | tf_op jit(solution)/shard_map/while/body/eval_jaxpr/all_to_all | solution.py:90
  79.3 4.7 collective-permute-start.3
  89.0 5.5 collective-permute-start.1
  107.1 12.7 %all-to-all-done = f32[32,1,960]{2,1,0:T(1,128)S(1)} async-done(((f32[32,1,960]{2,1,0:T(1,128)}), f32[32,1,960]{2,1,0:T(1,128)S(1)}, u32[]{:S(2)}, u32[]{:S(2)}) %all-to-all-start) | async-done | bytes 122912 | tf_op jit(solution)/shard_map/while/body/eval_jaxpr/all_to_all | solution.py:90
  140.8 6.1 %collective-permute-start.3 = (f32[4,3,1,1024]{3,2,0,1:T(1,128)S(1)}, f32[4,3,1,1024]{3,2,0,1:T(1,128)S(1)}, u32[]{:S(2)}, u32[]{:S(2)}) collective-permute-start(f32[4,3,1,1024]{3,2,0,1:T(1,128)S(1)} %get-tuple-element.313), channel_id=1, source_target_pairs={{0,1},{1,2},{2,3},{3,4},{4,5},{5,6},{6,7},{7,8},{8,9},{9,10},{10,1... | collective-permute-start | bytes 147464 | tf_op jit(solution)/shard_map/while/body/eval_jaxpr/ppermute | solution.py:20
  151.9 5.5 collective-permute-start.1
  169.9 13.2 %all-to-all-done = f32[32,1,960]{2,1,0:T(1,128)S(1)} async-done(((f32[32,1,960]{2,1,0:T(1,128)}), f32[32,1,960]{2,1,0:T(1,128)S(1)}, u32[]{:S(2)}, u32[]{:S(2)}) %all-to-all-start) | async-done | bytes 122912 | tf_op jit(solution)/shard_map/while/body/eval_jaxpr/all_to_all | solution.py:90
  204.1 5.6 collective-permute-start.3
  214.8 5.5 collective-permute-start.1
  232.8 12.7 %all-to-all-done = f32[32,1,960]{2,1,0:T(1,128)S(1)} async-done(((f32[32,1,960]{2,1,0:T(1,128)}), f32[32,1,960]{2,1,0:T(1,128)S(1)}, u32[]{:S(2)}, u32[]{:S(2)}) %all-to-all-start) | async-done | bytes 122912 | tf_op jit(solution)/shard_map/while/body/eval_jaxpr/all_to_all | solution.py:90
  266.5 4.9 collective-permute-start.3
  276.5 5.5 collective-permute-start.1
  294.5 13.4 %all-to-all-done = f32[32,1,960]{2,1,0:T(1,128)S(1)} async-done(((f32[32,1,960]{2,1,0:T(1,128)}), f32[32,1,960]{2,1,0:T(1,128)S(1)}, u32[]{:S(2)}, u32[]{:S(2)}) %all-to-all-start) | async-done | bytes 122912 | tf_op jit(solution)/shard_map/while/body/eval_jaxpr/all_to_all | solution.py:90
  328.9 4.9 collective-permute-start.3
  338.8 5.5 collective-permute-start.1
  356.8 12.7 %all-to-all-done = f32[32,1,960]{2,1,0:T(1,128)S(1)} async-done(((f32[32,1,960]{2,1,0:T(1,128)}), f32[32,1,960]{2,1,0:T(1,128)S(1)}, u32[]{:S(2)}, u32[]{:S(2)}) %all-to-all-start) | async-done | bytes 122912 | tf_op jit(solution)/shard_map/while/body/eval_jaxpr/all_to_all | solution.py:90
  390.6 4.9 collective-permute-start.3
  400.4 5.5 collective-permute-start.1
  418.5 12.7 %all-to-all-done = f32[32,1,960]{2,1,0:T(1,128)S(1)} async-done(((f32[32,1,960]{2,1,0:T(1,128)}), f32[32,1,960]{2,1,0:T(1,128)S(1)}, u32[]{:S(2)}, u32[]{:S(2)}) %all-to-all-start) | async-done | bytes 122912 | tf_op jit(solution)/shard_map/while/body/eval_jaxpr/all_to_all | solution.py:90
  452.2 4.9 collective-permute-start.3
  462.0 5.5 collective-permute-start.1
  480.4 12.7 %all-to-all-done = f32[32,1,960]{2,1,0:T(1,128)S(1)} async-done(((f32[32,1,960]{2,1,0:T(1,128)}), f32[32,1,960]{2,1,0:T(1,128)S(1)}, u32[]{:S(2)}, u32[]{:S(2)}) %all-to-all-start) | async-done | bytes 122912 | tf_op jit(solution)/shard_map/while/body/eval_jaxpr/all_to_all | solution.py:90
  514.2 4.9 collective-permute-start.3
  522.0 4.5 copy.87
  526.6 9.3 %reshape.90 = f32[32,1,3072]{2,1,0:T(1,128)} reshape(f32[1024,3,4,8]{3,2,1,0:T(4,128)} %bitcast.118) | data formatting | bytes 786432
  540.0 21.5 %all-to-all-done.1 = f32[32,1,3072]{2,1,0:T(1,128)S(1)} async-done(((f32[32,1,3072]{2,1,0:T(1,128)}), f32[32,1,3072]{2,1,0:T(1,128)S(1)}, u32[]{:S(2)}, u32[]{:S(2)}) %all-to-all-start.1) | async-done | bytes 393248 | tf_op jit(solution)/shard_map/all_to_all | solution.py:106
  563.6 9.2 %reshape.91 = f32[1024,3,4,8]{3,2,1,0:T(4,128)} reshape(f32[32,3072]{1,0:T(8,128)S(1)} %reduce.1) | data formatting | bytes 786432
  572.8 5.6 copy.88
  (594 shorter events, 303.8 us)
Async XLA Ops:
  0.9 9.6 %collective-permute-start.4 = (f32[8,3,1,32]{3,1,2,0:T(4,128)S(1)}, f32[8,3,1,32]{3,1,2,0:T(4,128)S(1)}, u32[]{:S(2)}, u32[]{:S(2)}) collective-permute-start(f32[8,3,1,32]{3,1,2,0:T(4,128)S(1)} %get-tuple-element.177), channel_id=1, source_target_pairs={{0,1},{1,2},{2,3},{3,4},{4,5},{5,6},{6,7},{7,8},{8,9},{9,10},{10,1... | collective-permute-start | bytes 9224 | tf_op jit(solution)/shard_map/ppermute | solution.py:20
  13.3 27.4 %collective-permute-start = (f32[4,3,1,1024]{3,2,0,1:T(1,128)S(1)}, f32[4,3,1,1024]{3,2,0,1:T(1,128)S(1)}, u32[]{:S(2)}, u32[]{:S(2)}) collective-permute-start(f32[4,3,1,1024]{3,2,0,1:T(1,128)S(1)} %get-tuple-element.273), channel_id=1, source_target_pairs={{1,0},{2,1},{3,2},{4,3},{5,4},{6,5},{7,6},{8,7},{9,8},{10,9},{11,1... | collective-permute-start | bytes 147464 | tf_op jit(solution)/shard_map/while/body/eval_jaxpr/ppermute | solution.py:22
  15.2 25.5 %collective-permute-start.1 = (f32[4,3,1,1024]{3,2,0,1:T(1,128)S(1)}, f32[4,3,1,1024]{3,2,0,1:T(1,128)S(1)}, u32[]{:S(2)}, u32[]{:S(2)}) collective-permute-start(f32[4,3,1,1024]{3,2,0,1:T(1,128)S(1)} %get-tuple-element.274), channel_id=1, source_target_pairs={{0,1},{1,2},{2,3},{3,4},{4,5},{5,6},{6,7},{7,8},{8,9},{9,10},{10,1... | collective-permute-start | bytes 147464 | tf_op jit(solution)/shard_map/while/body/eval_jaxpr/ppermute | solution.py:20
  25.2 32.9 %all-to-all-start = ((f32[32,1,960]{2,1,0:T(1,128)}), f32[32,1,960]{2,1,0:T(1,128)S(1)}, u32[]{:S(2)}, u32[]{:S(2)}) async-start(f32[32,1,960]{2,1,0:T(1,128)} %reshape.94), calls=%async_computation | async-start | bytes 262144 | tf_op jit(solution)/shard_map/while/body/eval_jaxpr/all_to_all | solution.py:90
  77.2 6.8 %collective-permute-start.2 = (f32[4,3,1,1024]{3,2,0,1:T(1,128)S(1)}, f32[4,3,1,1024]{3,2,0,1:T(1,128)S(1)}, u32[]{:S(2)}, u32[]{:S(2)}) collective-permute-start(f32[4,3,1,1024]{3,2,0,1:T(1,128)S(1)} %get-tuple-element.312), channel_id=1, source_target_pairs={{1,0},{2,1},{3,2},{4,3},{5,4},{6,5},{7,6},{8,7},{9,8},{10,9},{11,1... | collective-permute-start | bytes 147464 | tf_op jit(solution)/shard_map/while/body/eval_jaxpr/ppermute | solution.py:22
  87.1 16.4 %collective-permute-start = (f32[4,3,1,1024]{3,2,0,1:T(1,128)S(1)}, f32[4,3,1,1024]{3,2,0,1:T(1,128)S(1)}, u32[]{:S(2)}, u32[]{:S(2)}) collective-permute-start(f32[4,3,1,1024]{3,2,0,1:T(1,128)S(1)} %get-tuple-element.273), channel_id=1, source_target_pairs={{1,0},{2,1},{3,2},{4,3},{5,4},{6,5},{7,6},{8,7},{9,8},{10,9},{11,1... | collective-permute-start | bytes 147464 | tf_op jit(solution)/shard_map/while/body/eval_jaxpr/ppermute | solution.py:22
  89.0 14.5 %collective-permute-start.1 = (f32[4,3,1,1024]{3,2,0,1:T(1,128)S(1)}, f32[4,3,1,1024]{3,2,0,1:T(1,128)S(1)}, u32[]{:S(2)}, u32[]{:S(2)}) collective-permute-start(f32[4,3,1,1024]{3,2,0,1:T(1,128)S(1)} %get-tuple-element.274), channel_id=1, source_target_pairs={{0,1},{1,2},{2,3},{3,4},{4,5},{5,6},{6,7},{7,8},{8,9},{9,10},{10,1... | collective-permute-start | bytes 147464 | tf_op jit(solution)/shard_map/while/body/eval_jaxpr/ppermute | solution.py:20
  99.6 20.1 %all-to-all-start = ((f32[32,1,960]{2,1,0:T(1,128)}), f32[32,1,960]{2,1,0:T(1,128)S(1)}, u32[]{:S(2)}, u32[]{:S(2)}) async-start(f32[32,1,960]{2,1,0:T(1,128)} %reshape.94), calls=%async_computation | async-start | bytes 262144 | tf_op jit(solution)/shard_map/while/body/eval_jaxpr/all_to_all | solution.py:90
  138.8 8.0 %collective-permute-start.2 = (f32[4,3,1,1024]{3,2,0,1:T(1,128)S(1)}, f32[4,3,1,1024]{3,2,0,1:T(1,128)S(1)}, u32[]{:S(2)}, u32[]{:S(2)}) collective-permute-start(f32[4,3,1,1024]{3,2,0,1:T(1,128)S(1)} %get-tuple-element.312), channel_id=1, source_target_pairs={{1,0},{2,1},{3,2},{4,3},{5,4},{6,5},{7,6},{8,7},{9,8},{10,9},{11,1... | collective-permute-start | bytes 147464 | tf_op jit(solution)/shard_map/while/body/eval_jaxpr/ppermute | solution.py:22
  140.8 7.3 %collective-permute-start.3 = (f32[4,3,1,1024]{3,2,0,1:T(1,128)S(1)}, f32[4,3,1,1024]{3,2,0,1:T(1,128)S(1)}, u32[]{:S(2)}, u32[]{:S(2)}) collective-permute-start(f32[4,3,1,1024]{3,2,0,1:T(1,128)S(1)} %get-tuple-element.313), channel_id=1, source_target_pairs={{0,1},{1,2},{2,3},{3,4},{4,5},{5,6},{6,7},{7,8},{8,9},{9,10},{10,1... | collective-permute-start | bytes 147464 | tf_op jit(solution)/shard_map/while/body/eval_jaxpr/ppermute | solution.py:20
  150.0 16.4 %collective-permute-start = (f32[4,3,1,1024]{3,2,0,1:T(1,128)S(1)}, f32[4,3,1,1024]{3,2,0,1:T(1,128)S(1)}, u32[]{:S(2)}, u32[]{:S(2)}) collective-permute-start(f32[4,3,1,1024]{3,2,0,1:T(1,128)S(1)} %get-tuple-element.273), channel_id=1, source_target_pairs={{1,0},{2,1},{3,2},{4,3},{5,4},{6,5},{7,6},{8,7},{9,8},{10,9},{11,1... | collective-permute-start | bytes 147464 | tf_op jit(solution)/shard_map/while/body/eval_jaxpr/ppermute | solution.py:22
  151.9 14.5 %collective-permute-start.1 = (f32[4,3,1,1024]{3,2,0,1:T(1,128)S(1)}, f32[4,3,1,1024]{3,2,0,1:T(1,128)S(1)}, u32[]{:S(2)}, u32[]{:S(2)}) collective-permute-start(f32[4,3,1,1024]{3,2,0,1:T(1,128)S(1)} %get-tuple-element.274), channel_id=1, source_target_pairs={{0,1},{1,2},{2,3},{3,4},{4,5},{5,6},{6,7},{7,8},{8,9},{9,10},{10,1... | collective-permute-start | bytes 147464 | tf_op jit(solution)/shard_map/while/body/eval_jaxpr/ppermute | solution.py:20
  162.5 20.6 %all-to-all-start = ((f32[32,1,960]{2,1,0:T(1,128)}), f32[32,1,960]{2,1,0:T(1,128)S(1)}, u32[]{:S(2)}, u32[]{:S(2)}) async-start(f32[32,1,960]{2,1,0:T(1,128)} %reshape.94), calls=%async_computation | async-start | bytes 262144 | tf_op jit(solution)/shard_map/while/body/eval_jaxpr/all_to_all | solution.py:90
  202.2 7.5 %collective-permute-start.2 = (f32[4,3,1,1024]{3,2,0,1:T(1,128)S(1)}, f32[4,3,1,1024]{3,2,0,1:T(1,128)S(1)}, u32[]{:S(2)}, u32[]{:S(2)}) collective-permute-start(f32[4,3,1,1024]{3,2,0,1:T(1,128)S(1)} %get-tuple-element.312), channel_id=1, source_target_pairs={{1,0},{2,1},{3,2},{4,3},{5,4},{6,5},{7,6},{8,7},{9,8},{10,9},{11,1... | collective-permute-start | bytes 147464 | tf_op jit(solution)/shard_map/while/body/eval_jaxpr/ppermute | solution.py:22
  212.8 16.4 %collective-permute-start = (f32[4,3,1,1024]{3,2,0,1:T(1,128)S(1)}, f32[4,3,1,1024]{3,2,0,1:T(1,128)S(1)}, u32[]{:S(2)}, u32[]{:S(2)}) collective-permute-start(f32[4,3,1,1024]{3,2,0,1:T(1,128)S(1)} %get-tuple-element.273), channel_id=1, source_target_pairs={{1,0},{2,1},{3,2},{4,3},{5,4},{6,5},{7,6},{8,7},{9,8},{10,9},{11,1... | collective-permute-start | bytes 147464 | tf_op jit(solution)/shard_map/while/body/eval_jaxpr/ppermute | solution.py:22
  214.8 14.5 %collective-permute-start.1 = (f32[4,3,1,1024]{3,2,0,1:T(1,128)S(1)}, f32[4,3,1,1024]{3,2,0,1:T(1,128)S(1)}, u32[]{:S(2)}, u32[]{:S(2)}) collective-permute-start(f32[4,3,1,1024]{3,2,0,1:T(1,128)S(1)} %get-tuple-element.274), channel_id=1, source_target_pairs={{0,1},{1,2},{2,3},{3,4},{4,5},{5,6},{6,7},{7,8},{8,9},{9,10},{10,1... | collective-permute-start | bytes 147464 | tf_op jit(solution)/shard_map/while/body/eval_jaxpr/ppermute | solution.py:20
  225.3 20.1 %all-to-all-start = ((f32[32,1,960]{2,1,0:T(1,128)}), f32[32,1,960]{2,1,0:T(1,128)S(1)}, u32[]{:S(2)}, u32[]{:S(2)}) async-start(f32[32,1,960]{2,1,0:T(1,128)} %reshape.94), calls=%async_computation | async-start | bytes 262144 | tf_op jit(solution)/shard_map/while/body/eval_jaxpr/all_to_all | solution.py:90
  264.6 6.9 %collective-permute-start.2 = (f32[4,3,1,1024]{3,2,0,1:T(1,128)S(1)}, f32[4,3,1,1024]{3,2,0,1:T(1,128)S(1)}, u32[]{:S(2)}, u32[]{:S(2)}) collective-permute-start(f32[4,3,1,1024]{3,2,0,1:T(1,128)S(1)} %get-tuple-element.312), channel_id=1, source_target_pairs={{1,0},{2,1},{3,2},{4,3},{5,4},{6,5},{7,6},{8,7},{9,8},{10,9},{11,1... | collective-permute-start | bytes 147464 | tf_op jit(solution)/shard_map/while/body/eval_jaxpr/ppermute | solution.py:22
  274.5 16.4 %collective-permute-start = (f32[4,3,1,1024]{3,2,0,1:T(1,128)S(1)}, f32[4,3,1,1024]{3,2,0,1:T(1,128)S(1)}, u32[]{:S(2)}, u32[]{:S(2)}) collective-permute-start(f32[4,3,1,1024]{3,2,0,1:T(1,128)S(1)} %get-tuple-element.273), channel_id=1, source_target_pairs={{1,0},{2,1},{3,2},{4,3},{5,4},{6,5},{7,6},{8,7},{9,8},{10,9},{11,1... | collective-permute-start | bytes 147464 | tf_op jit(solution)/shard_map/while/body/eval_jaxpr/ppermute | solution.py:22
  276.5 14.5 %collective-permute-start.1 = (f32[4,3,1,1024]{3,2,0,1:T(1,128)S(1)}, f32[4,3,1,1024]{3,2,0,1:T(1,128)S(1)}, u32[]{:S(2)}, u32[]{:S(2)}) collective-permute-start(f32[4,3,1,1024]{3,2,0,1:T(1,128)S(1)} %get-tuple-element.274), channel_id=1, source_target_pairs={{0,1},{1,2},{2,3},{3,4},{4,5},{5,6},{6,7},{7,8},{8,9},{9,10},{10,1... | collective-permute-start | bytes 147464 | tf_op jit(solution)/shard_map/while/body/eval_jaxpr/ppermute | solution.py:20
  287.0 20.8 %all-to-all-start = ((f32[32,1,960]{2,1,0:T(1,128)}), f32[32,1,960]{2,1,0:T(1,128)S(1)}, u32[]{:S(2)}, u32[]{:S(2)}) async-start(f32[32,1,960]{2,1,0:T(1,128)} %reshape.94), calls=%async_computation | async-start | bytes 262144 | tf_op jit(solution)/shard_map/while/body/eval_jaxpr/all_to_all | solution.py:90
  327.0 6.8 %collective-permute-start.2 = (f32[4,3,1,1024]{3,2,0,1:T(1,128)S(1)}, f32[4,3,1,1024]{3,2,0,1:T(1,128)S(1)}, u32[]{:S(2)}, u32[]{:S(2)}) collective-permute-start(f32[4,3,1,1024]{3,2,0,1:T(1,128)S(1)} %get-tuple-element.312), channel_id=1, source_target_pairs={{1,0},{2,1},{3,2},{4,3},{5,4},{6,5},{7,6},{8,7},{9,8},{10,9},{11,1... | collective-permute-start | bytes 147464 | tf_op jit(solution)/shard_map/while/body/eval_jaxpr/ppermute | solution.py:22
  336.9 16.4 %collective-permute-start = (f32[4,3,1,1024]{3,2,0,1:T(1,128)S(1)}, f32[4,3,1,1024]{3,2,0,1:T(1,128)S(1)}, u32[]{:S(2)}, u32[]{:S(2)}) collective-permute-start(f32[4,3,1,1024]{3,2,0,1:T(1,128)S(1)} %get-tuple-element.273), channel_id=1, source_target_pairs={{1,0},{2,1},{3,2},{4,3},{5,4},{6,5},{7,6},{8,7},{9,8},{10,9},{11,1... | collective-permute-start | bytes 147464 | tf_op jit(solution)/shard_map/while/body/eval_jaxpr/ppermute | solution.py:22
  338.8 14.5 %collective-permute-start.1 = (f32[4,3,1,1024]{3,2,0,1:T(1,128)S(1)}, f32[4,3,1,1024]{3,2,0,1:T(1,128)S(1)}, u32[]{:S(2)}, u32[]{:S(2)}) collective-permute-start(f32[4,3,1,1024]{3,2,0,1:T(1,128)S(1)} %get-tuple-element.274), channel_id=1, source_target_pairs={{0,1},{1,2},{2,3},{3,4},{4,5},{5,6},{6,7},{7,8},{8,9},{9,10},{10,1... | collective-permute-start | bytes 147464 | tf_op jit(solution)/shard_map/while/body/eval_jaxpr/ppermute | solution.py:20
  349.4 20.1 %all-to-all-start = ((f32[32,1,960]{2,1,0:T(1,128)}), f32[32,1,960]{2,1,0:T(1,128)S(1)}, u32[]{:S(2)}, u32[]{:S(2)}) async-start(f32[32,1,960]{2,1,0:T(1,128)} %reshape.94), calls=%async_computation | async-start | bytes 262144 | tf_op jit(solution)/shard_map/while/body/eval_jaxpr/all_to_all | solution.py:90
  398.5 16.4 %collective-permute-start = (f32[4,3,1,1024]{3,2,0,1:T(1,128)S(1)}, f32[4,3,1,1024]{3,2,0,1:T(1,128)S(1)}, u32[]{:S(2)}, u32[]{:S(2)}) collective-permute-start(f32[4,3,1,1024]{3,2,0,1:T(1,128)S(1)} %get-tuple-element.273), channel_id=1, source_target_pairs={{1,0},{2,1},{3,2},{4,3},{5,4},{6,5},{7,6},{8,7},{9,8},{10,9},{11,1... | collective-permute-start | bytes 147464 | tf_op jit(solution)/shard_map/while/body/eval_jaxpr/ppermute | solution.py:22
  400.4 14.5 %collective-permute-start.1 = (f32[4,3,1,1024]{3,2,0,1:T(1,128)S(1)}, f32[4,3,1,1024]{3,2,0,1:T(1,128)S(1)}, u32[]{:S(2)}, u32[]{:S(2)}) collective-permute-start(f32[4,3,1,1024]{3,2,0,1:T(1,128)S(1)} %get-tuple-element.274), channel_id=1, source_target_pairs={{0,1},{1,2},{2,3},{3,4},{4,5},{5,6},{6,7},{7,8},{8,9},{9,10},{10,1... | collective-permute-start | bytes 147464 | tf_op jit(solution)/shard_map/while/body/eval_jaxpr/ppermute | solution.py:20
  411.0 20.1 %all-to-all-start = ((f32[32,1,960]{2,1,0:T(1,128)}), f32[32,1,960]{2,1,0:T(1,128)S(1)}, u32[]{:S(2)}, u32[]{:S(2)}) async-start(f32[32,1,960]{2,1,0:T(1,128)} %reshape.94), calls=%async_computation | async-start | bytes 262144 | tf_op jit(solution)/shard_map/while/body/eval_jaxpr/all_to_all | solution.py:90
  460.1 16.7 %collective-permute-start = (f32[4,3,1,1024]{3,2,0,1:T(1,128)S(1)}, f32[4,3,1,1024]{3,2,0,1:T(1,128)S(1)}, u32[]{:S(2)}, u32[]{:S(2)}) collective-permute-start(f32[4,3,1,1024]{3,2,0,1:T(1,128)S(1)} %get-tuple-element.273), channel_id=1, source_target_pairs={{1,0},{2,1},{3,2},{4,3},{5,4},{6,5},{7,6},{8,7},{9,8},{10,9},{11,1... | collective-permute-start | bytes 147464 | tf_op jit(solution)/shard_map/while/body/eval_jaxpr/ppermute | solution.py:22
  462.0 14.8 %collective-permute-start.1 = (f32[4,3,1,1024]{3,2,0,1:T(1,128)S(1)}, f32[4,3,1,1024]{3,2,0,1:T(1,128)S(1)}, u32[]{:S(2)}, u32[]{:S(2)}) collective-permute-start(f32[4,3,1,1024]{3,2,0,1:T(1,128)S(1)} %get-tuple-element.274), channel_id=1, source_target_pairs={{0,1},{1,2},{2,3},{3,4},{4,5},{5,6},{6,7},{7,8},{8,9},{9,10},{10,1... | collective-permute-start | bytes 147464 | tf_op jit(solution)/shard_map/while/body/eval_jaxpr/ppermute | solution.py:20
  472.6 20.5 %all-to-all-start = ((f32[32,1,960]{2,1,0:T(1,128)}), f32[32,1,960]{2,1,0:T(1,128)S(1)}, u32[]{:S(2)}, u32[]{:S(2)}) async-start(f32[32,1,960]{2,1,0:T(1,128)} %reshape.94), calls=%async_computation | async-start | bytes 262144 | tf_op jit(solution)/shard_map/while/body/eval_jaxpr/all_to_all | solution.py:90
  535.9 25.6 %all-to-all-start.1 = ((f32[32,1,3072]{2,1,0:T(1,128)}), f32[32,1,3072]{2,1,0:T(1,128)S(1)}, u32[]{:S(2)}, u32[]{:S(2)}) async-start(f32[32,1,3072]{2,1,0:T(1,128)} %reshape.90), calls=%async_computation.1 | async-start | bytes 786432 | tf_op jit(solution)/shard_map/all_to_all | solution.py:106
  (61 other events, 772.9 us)
